TPU v7x, 32 devices: a whole 2x2x4 slice. The times are simulated.
32 devices in a mesh: dp: 16 (over z, y, x), clus: 2 (over core).
Axes of the slice: x: 2, y: 2, z: 4, core: 2. Of those that a mesh axis runs over, the one named last changes fastest.
Arguments:
- embeddings: bfloat16 [8192, 4096], P('dp'), may hold values from -6 to 6
- assignment: int32 [8192], P('dp'), may hold values from 0 to 95
- slot_of: int32 [96], replicated, may hold values from 0 to 95, each once
- old_centroids: bfloat16 [96, 4096], P(('clus', 'dp')), may hold values from -6 to 6
Outputs:
- new_centroids: float32 [96, 4096], P(('clus', 'dp'))
- distance: float32 [8192], P('dp')
All inputs are finite; a program needn't handle non-finite values.
Results may differ from a plain program's by a relative error of at most 0.0003.
Values may be sent and summed in bfloat16 or wider, within the bound.
A program may use at most 64 MiB of HBM per device.

v0:
```python
import jax
import jax.numpy as jnp
from jax import lax
from jax.sharding import PartitionSpec as P

D = 4096


def per_device(embeddings, assignment, slot_of, old_centroids):
    rows_own = old_centroids.shape[0]
    block_rows = rows_own * lax.axis_size("dp")
    clusters = slot_of.shape[0]
    first_slot = lax.axis_index("clus") * block_rows
    matches = assignment[:, None] == jnp.arange(clusters, dtype=jnp.int32)[None, :]
    slot_ids = jnp.sum(jnp.where(matches, slot_of[None, :], 0), axis=1)
    local_ids = slot_ids - first_slot
    one_hot = (jnp.arange(block_rows, dtype=jnp.int32)[:, None] == local_ids[None, :]).astype(
        jnp.bfloat16
    )
    shard_rows = lax.all_gather(old_centroids, "dp", axis=0, tiled=True)
    raw = lax.dot_general(
        shard_rows, embeddings, (((1,), (1,)), ((), ())), preferred_element_type=jnp.float32
    )
    cent_wide = shard_rows.astype(jnp.float32)
    cent_rms = jnp.sqrt(jnp.mean(cent_wide * cent_wide, axis=1, keepdims=True) + 1e-06)
    scores = raw / cent_rms
    picked = jnp.sum(one_hot.astype(jnp.float32) * scores, axis=0)
    widened = embeddings.astype(jnp.float32)
    root_mean = jnp.sqrt(jnp.mean(widened * widened, axis=1) + 1e-06)
    partial_value = picked / (jnp.float32(D) * root_mean)
    overall_scores = lax.psum(partial_value, "clus")
    distance = 1.0 - overall_scores
    block_sums = jnp.dot(one_hot, embeddings, preferred_element_type=jnp.float32)
    all_sums = lax.psum(block_sums, "dp")
    own_sums = lax.dynamic_slice_in_dim(all_sums, lax.axis_index("dp") * rows_own, rows_own, 0)
    overall = own_sums + old_centroids.astype(jnp.float32)
    updated = overall * lax.rsqrt(jnp.mean(overall * overall, axis=1, keepdims=True) + 1e-06)
    return (updated, distance)


def solution(mesh):
    in_specs = (P("dp", None), P("dp"), P(), P(("clus", "dp"), None))
    out_specs = (P(("clus", "dp"), None), P("dp"))
    return jax.shard_map(
        per_device, mesh=mesh, in_specs=in_specs, out_specs=out_specs, check_vma=False
    )
```

profile of v0, /device:TPU:0, one launch (start us, length us, event | category | flops | bytes accessed | tf_op | source)
XLA Modules:
  0.0 136.9 jit_solution(8602947187259082100)
XLA Ops:
  7.2 0.0 all-reduce.2.cloned.1.call-start
  7.2 0.8 select_reduce_fusion
  8.0 0.0 copy-start
  8.0 3.9 %fusion.3 = f32[48,4096]{1,0:T(8,128)} fusion(bf16[512,4096]{1,0:T(8,128)(2,1)} %param.4, s32[512]{0:T(512)S(1)} %broadcast_subtract_fusion.1), kind=kOutput, calls=%fused_computation.9 | convolution fusion | flops 201351168 | bytes 4982784 | tf_op jit(solution)/shard_map/dot_general | solution.py:33
  12.0 0.0 all-reduce.2.cloned.1.call-update
  12.0 3.1 %multiply_reduce_fusion = f32[512]{0:T(512)S(1)} fusion(bf16[512,4096]{1,0:T(8,128)(2,1)} %param.4), kind=kLoop, calls=%fused_computation | loop fusion | flops 6290944 | bytes 4196352 | tf_op jit(solution)/shard_map/reduce_sum | solution.py:29
  15.1 0.0 copy-done
  15.1 46.2 %all-gather = bf16[16,3,4096]{2,1,0:T(4,128)(2,1)S(1)} all-gather(bf16[1,3,4096]{2,1,0:T(4,128)(2,1)S(1)} %bitcast.4), channel_id=1, replica_groups=mesh['dp'=16,'clus'=2] {'dp'}, dimensions={0}, use_global_device_ids=true | all-gather | bytes 417792 | tf_op jit(solution)/shard_map/all_gather | solution.py:20
  61.3 0.3 reshape.26
  61.7 0.2 multiply_reduce_fusion.1
  61.9 3.6 %fusion.1 = f32[512]{0:T(512)S(1)} fusion(bf16[48,4096]{1,0:T(8,128)(2,1)S(1)} %reshape.26, bf16[512,4096]{1,0:T(8,128)(2,1)} %param.4, f32[48]{0:T(128)S(1)} %add_sqrt_fusion, s32[512]{0:T(512)S(1)} %broadcast_subtract_fusion.1), kind=kOutput, calls=%fused_computation.3 | convolution fusion | flops 201473536 | bytes 4591808 | tf_op jit(solution)/shard_map/dot_general | solution.py:21
  65.5 2.5 %psum.15 = f32[512]{0:T(512)S(1)} all-reduce(f32[512]{0:T(512)S(1)} %multiply_divide_fusion), channel_id=1, replica_groups=mesh['dp'=16,'clus'=2] {'clus'}, use_global_device_ids=true, to_apply=%region_6.7 | all-reduce | flops 512 | bytes 4096 | tf_op jit(solution)/shard_map/psum | solution.py:31
  68.0 0.6 broadcast_subtract_fusion
  68.5 58.8 %all-reduce.2.cloned.1.call-done = f32[48,4096]{1,0:T(8,128)} async-done(((f32[48,4096]{1,0:T(8,128)}), f32[48,4096]{1,0:T(8,128)}) %all-reduce.2.cloned.1.call-update) | async-done | bytes 786448 | tf_op jit(solution)/shard_map/psum | solution.py:34
  127.3 1.1 multiply_reduce_fusion.2
  128.4 1.7 %fusion.5 = f32[3,4096]{1,0:T(4,128)} fusion(bf16[3,4096]{1,0:T(4,128)(2,1)S(1)} %copy-done, f32[48,4096]{1,0:T(8,128)} %all-reduce.2.cloned.1.call-done, s32[]{:T(128)S(6)} %select_n.8, f32[3]{0:T(128)S(1)} %add_rsqrt_fusion), kind=kLoop, calls=%fused_computation.13 | loop fusion | flops 36864 | bytes 122896 | tf_op jit(solution)/shard_map/mul | solution.py:37
  (4 shorter events, 0.0 us)
Async XLA Ops:
  7.2 120.1 %all-reduce.2.cloned.1.call-start = ((), (), s32[]{:S(2)}) async-start(), calls=%async_computation | async-start | bytes 1572864 | tf_op jit(solution)/shard_map/psum | solution.py:34
  8.0 7.1 %copy-start = (bf16[3,4096]{1,0:T(4,128)(2,1)S(1)}, bf16[3,4096]{1,0:T(4,128)(2,1)}, u32[]{:S(2)}) copy-start(bf16[3,4096]{1,0:T(4,128)(2,1)} %param.7) | copy-start | bytes 73732
Sparse Core Ops, SparseCore 0:
  13.2 114.0 all-reduce.1
where the time goes:
time: 137 us
  waiting for transfers between devices  58.8 us (43%)
  blocking collectives  48.7 us (36%)
  between operations  14.1 us (10%)
  matrix products  7.54 us (6%)
  other arithmetic  7.46 us (5%)
    psum x1, waiting for transfers between devices, per_device(): all_sums = lax.psum(block_sums, 'dp')  58.8 us
    all_gather x1, blocking collectives, per_device(): shard_rows = lax.all_gather(old_centroids, 'dp', axis=0, tiled=True)  46.2 us
    dot_general x1, matrix products, per_device(): jnp.dot(one_hot, embeddings, preferred_element_type=jnp.float32)  3.93 us
    dot_general x1, matrix products, per_device(): lax.dot_general(shard_rows, embeddings, (((1,), (1,)), ((), ())), preferr...  3.61 us
    reduce_sum x1, other arithmetic, per_device(): root_mean = jnp.sqrt(jnp.mean(widened * widened, axis=1) + 1e-06)  3.08 us
  transfers between devices with their start and end apart: 1, of which 1 were waited for; matrix products, arithmetic and copies ran while one was open for 6% of the time, Pallas kernels for 0%

commit v1 on v0

v1 whole, which is shorter than its diff:
```python
import functools

import jax
import jax.numpy as jnp
from jax import lax
from jax.experimental import pallas as pl
from jax.experimental.pallas import tpu as pltpu
from jax.sharding import PartitionSpec as P

LANES = 128
EPS = 1e-06


def inner_size(n):
    g = 1
    while n % (g * 2) == 0 and (g * 2) * (g * 2) <= n:
        g *= 2
    return g


def kernel(
    n, g, n_clus, nc,
    emb_hbm, asg_ref, slot_ref, cent_ref, new_ref, dist_ref,
    emb, sums, recv1, part, recv2, fin, cent_own, cent, cent_wide, cent_mat, sq, mine, theirs,
    emb_sem, s1_send, s1_recv, s2_send, s2_recv, g1_send, g1_recv, g2_send, g2_recv, x_send, x_recv,
):
    big = n // g
    rows, width = cent_ref.shape
    points = emb.shape[0]
    clusters = slot_ref.shape[1]
    block = n * rows
    tiles = width // LANES
    kc = tiles // nc
    cw = kc * LANES
    me = lax.axis_index("dp")
    own_clus = lax.axis_index("clus")
    zo, p = me // g, me % g

    def device(dp):
        return {"dp": dp}

    loads = []
    for c in range(nc):
        cols = pl.ds(c * cw, cw)
        cp = pltpu.make_async_copy(emb_hbm.at[:, cols], emb.at[:, cols], emb_sem.at[c])
        cp.start()
        loads.append(cp)

    inner = [zo * g + lax.rem(p + j, g) for j in range(1, g)]
    outer = [lax.rem(zo + i, big) * g + p for i in range(1, big)]
    partners = [lax.rem(own_clus + q, n_clus) for q in range(1, n_clus)]

    barrier = pltpu.get_barrier_semaphore()
    for d in inner + outer:
        pl.semaphore_signal(barrier, inc=1, device_id=device(d), device_id_type=pl.DeviceIdType.MESH)
    for q in partners:
        pl.semaphore_signal(barrier, inc=1, device_id={"clus": q}, device_id_type=pl.DeviceIdType.MESH)

    def remote(src, dst, send, recv, where):
        cp = pltpu.make_async_remote_copy(
            src_ref=src, dst_ref=dst, send_sem=send, recv_sem=recv,
            device_id=where, device_id_type=pl.DeviceIdType.MESH,
        )
        cp.start()
        return cp

    old = cent_ref[...].astype(jnp.float32)
    for k in range(tiles):
        cent_own[pl.ds(k, rows, stride=tiles), :] = old[:, k * LANES:(k + 1) * LANES]
    cent[p, zo] = cent_own[...].astype(jnp.bfloat16)

    j = lax.broadcasted_iota(jnp.int32, (block, clusters), 0)
    local = ((j // rows) % big * g + j // (rows * big)) * rows + j % rows
    place = (slot_ref[...] == local + own_clus * block).astype(jnp.float32).astype(jnp.bfloat16)
    which = (
        lax.broadcasted_iota(jnp.int32, (clusters, points), 0) == asg_ref[...]
    ).astype(jnp.float32).astype(jnp.bfloat16)
    hot_wide = jnp.dot(place, which, preferred_element_type=jnp.float32)
    hot = hot_wide.astype(jnp.bfloat16)

    pl.semaphore_wait(barrier, len(inner) + len(outer) + len(partners))

    started = []
    gather1 = [
        remote(cent.at[p, zo], cent.at[p, zo], g1_send.at[i], g1_recv.at[i], device(d))
        for i, d in enumerate(outer)
    ]

    span = big * rows * kc
    step1 = []
    for c in range(nc):
        loads[c].wait()
        value = jnp.dot(hot, emb[:, c * cw:(c + 1) * cw], preferred_element_type=jnp.float32)
        for k in range(kc):
            sums[pl.ds(c * block * kc + k, block, stride=kc), :] = value[:, k * LANES:(k + 1) * LANES]
        copies = []
        for i, d in enumerate(inner):
            start = pl.multiple_of(c * block * kc + lax.rem(p + i + 1, g) * span, 8)
            copies.append(
                remote(sums.at[pl.ds(start, span)], recv1.at[c, i], s1_send.at[c, i], s1_recv.at[c, i], device(d))
            )
        step1.append(copies)
        x = emb[:, c * cw:(c + 1) * cw].astype(jnp.float32)
        x = x * x
        acc = x[:, :LANES]
        for k in range(1, kc):
            acc = acc + x[:, k * LANES:(k + 1) * LANES]
        if c == 0:
            sq[...] = acc
        else:
            sq[...] += acc

    for cp in gather1:
        cp.wait_recv()
    gather2 = [
        remote(cent.at[p], cent.at[p], g2_send.at[i], g2_recv.at[i], device(d))
        for i, d in enumerate(inner)
    ]

    sub = rows * kc
    step2 = []
    for c in range(nc):
        for cp in step1[c]:
            cp.wait_recv()
        start = pl.multiple_of(c * block * kc + p * span, 8)
        total = sums[pl.ds(start, span), :]
        for i in range(g - 1):
            total = total + recv1[c, i]
        part[c] = total.reshape(big, sub, LANES)
        step2.append([
            remote(
                part.at[c, lax.rem(zo + i + 1, big)], recv2.at[c, i],
                s2_send.at[c, i], s2_recv.at[c, i], device(d),
            )
            for i, d in enumerate(outer)
        ])

    ones = jnp.ones((8, LANES), jnp.float32)
    sumsq = lax.dot_general(
        ones, sq[...], (((1,), (1,)), ((), ())),
        preferred_element_type=jnp.float32, precision=lax.Precision.HIGHEST,
    )[:1]
    root_mean = jnp.sqrt(sumsq / width + EPS)

    for cp in gather2:
        cp.wait_recv()
    wide = cent[...].astype(jnp.float32).reshape(block * tiles, LANES)
    cent_wide[...] = wide
    cent_sq = jnp.sum(
        jnp.sum((wide * wide).reshape(block, tiles, LANES), axis=1), axis=1, keepdims=True
    )
    cent_rms = jnp.sqrt(cent_sq / width + EPS)
    for k in range(tiles):
        cent_mat[:, k * LANES:(k + 1) * LANES] = cent_wide[
            pl.ds(k, block, stride=tiles), :
        ].astype(jnp.bfloat16)
    raw = lax.dot_general(
        cent_mat[...], emb[...], (((1,), (1,)), ((), ())), preferred_element_type=jnp.float32
    )
    picked = jnp.sum(hot_wide * (raw / cent_rms), axis=0, keepdims=True)
    share = picked / (jnp.float32(width) * root_mean)
    mine[...] = jnp.broadcast_to(share, mine.shape)
    swap = [
        remote(mine, theirs.at[i], x_send.at[i], x_recv.at[i], {"clus": q})
        for i, q in enumerate(partners)
    ]

    for c in range(nc):
        for cp in step2[c]:
            cp.wait_recv()
        total = part[c, zo]
        for i in range(big - 1):
            total = total + recv2[c, i]
        fin[pl.ds(c * sub, sub), :] = total
    for c in range(nc):
        for k in range(kc):
            t = (c * kc + k) * LANES
            new_ref[:, t:t + LANES] = fin[pl.ds(c * sub + k, rows, stride=kc), :] + old[:, t:t + LANES]
    overall = new_ref[...]
    new_ref[...] = overall * lax.rsqrt(jnp.mean(overall * overall, axis=1, keepdims=True) + EPS)

    score = mine[:1]
    for i, cp in enumerate(swap):
        cp.wait_recv()
        score = score + theirs[i, :1]
    dist_ref[...] = 1.0 - score

    for cp in gather1 + gather2 + swap + sum(step1, []) + sum(step2, []):
        cp.wait_send()


def per_device(n, n_clus, embeddings, assignment, slot_of, old_centroids):
    points, width = embeddings.shape
    rows = old_centroids.shape[0]
    clusters = slot_of.shape[0]
    g = inner_size(n)
    big = n // g
    block = n * rows
    tiles = width // LANES
    nc = 4
    kc = tiles // nc
    dma = pltpu.SemaphoreType.DMA
    vmem = pl.BlockSpec(memory_space=pltpu.VMEM)
    new, dist = pl.pallas_call(
        functools.partial(kernel, n, g, n_clus, nc),
        out_shape=(
            jax.ShapeDtypeStruct((rows, width), jnp.float32),
            jax.ShapeDtypeStruct((1, points), jnp.float32),
        ),
        in_specs=[pl.BlockSpec(memory_space=pl.ANY), vmem, vmem, vmem],
        out_specs=(vmem, vmem),
        scratch_shapes=[
            pltpu.VMEM((points, width), embeddings.dtype),
            pltpu.VMEM((block * tiles, LANES), jnp.float32),
            pltpu.VMEM((nc, g - 1, big * rows * kc, LANES), jnp.float32),
            pltpu.VMEM((nc, big, rows * kc, LANES), jnp.float32),
            pltpu.VMEM((nc, big - 1, rows * kc, LANES), jnp.float32),
            pltpu.VMEM((rows * tiles, LANES), jnp.float32),
            pltpu.VMEM((rows * tiles, LANES), jnp.float32),
            pltpu.VMEM((g, big, rows * tiles, LANES), jnp.bfloat16),
            pltpu.VMEM((block * tiles, LANES), jnp.float32),
            pltpu.VMEM((block, width), jnp.bfloat16),
            pltpu.VMEM((points, LANES), jnp.float32),
            pltpu.VMEM((8, points), jnp.float32),
            pltpu.VMEM((n_clus - 1, 8, points), jnp.float32),
            dma((nc,)),
            dma((nc, g - 1)), dma((nc, g - 1)),
            dma((nc, big - 1)), dma((nc, big - 1)),
            dma((big - 1,)), dma((big - 1,)),
            dma((g - 1,)), dma((g - 1,)),
            dma((n_clus - 1,)), dma((n_clus - 1,)),
        ],
        compiler_params=pltpu.CompilerParams(
            collective_id=0, has_side_effects=True, vmem_limit_bytes=48 * 1024 * 1024
        ),
    )(embeddings, assignment.reshape(1, points), slot_of.reshape(1, clusters), old_centroids)
    return new, dist.reshape(points)


def solution(mesh):
    in_specs = (P("dp", None), P("dp"), P(), P(("clus", "dp"), None))
    out_specs = (P(("clus", "dp"), None), P("dp"))
    return jax.shard_map(
        functools.partial(per_device, mesh.shape["dp"], mesh.shape["clus"]),
        mesh=mesh, in_specs=in_specs, out_specs=out_specs, check_vma=False,
    )
```

time: 137 us -> 30.5 us (0.22)
  waiting for transfers between devices: 58.8 us -> 0 us
  blocking collectives: 48.7 us -> 0 us
  Pallas kernels: 0 us -> 24.1 us
  between operations: 14.1 us -> 0.65 us
  matrix products: 7.54 us -> 0 us
  other arithmetic: 7.46 us -> 0 us
  local copies, waits for them, and re-layouts: 0.34 us -> 5.48 us
    psum x1 -> x0, waiting for transfers between devices: 58.8 us -> none  [per_device(): all_sums = lax.psum(block_sums, 'dp')]
    all_gather x1 -> x0, blocking collectives: 46.2 us -> none  [per_device(): shard_rows = lax.all_gather(old_centroids, 'dp', axis=0, tiled=True)]
    pallas_call x0 -> x1, Pallas kernels: none -> 24.1 us  [per_device(): pl.pallas_call(functools.partial(kernel, n, g, n_clus, nc), out_shape=(ja...]
    dot_general x2 -> x0, matrix products: 7.54 us -> none  [the longest x1 3.93 us: per_device(): jnp.dot(one_hot, embeddings, preferred_element_type=jnp.float32)]
    reduce_sum x4 -> x0, other arithmetic: 5.17 us -> none  [the longest x1 3.08 us: per_device(): root_mean = jnp.sqrt(jnp.mean(widened * widened, axis=1) + 1e-06)]
    unnamed x3 -> x10, local copies, waits for them, and re-layouts: 0.34 us -> 5.48 us
    psum x1 -> x0, blocking collectives: 2.47 us -> none  [per_device(): overall_scores = lax.psum(partial_value, 'clus')]
    mul x1 -> x0, other arithmetic: 1.66 us -> none  [per_device(): overall * lax.rsqrt(jnp.mean(overall * overall, axis=1, keepdims=True) +...]
  transfers between devices with their start and end apart: 1 -> 0, of which waited for: 1 -> 0; matrix products, arithmetic and copies ran while one was open for 6% -> 0% of each run, Pallas kernels for 0% -> 0%
where the time goes in v1:
time: 30.5 us; the launch traced here: 30.3 us
  Pallas kernels  24.1 us (79%)
  local copies, waits for them, and re-layouts  5.48 us (18%)
  between operations  0.65 us (2%)
    pallas_call x1, Pallas kernels, per_device(): pl.pallas_call(functools.partial(kernel, n, g, n_clus, nc), out_shape=(ja...  24.1 us
    unnamed x10, local copies, waits for them, and re-layouts  5.48 us

profile of v1, /device:TPU:0, one launch (start us, length us, event | category | flops | bytes accessed | tf_op | source)
XLA Modules:
  0.0 30.3 jit_solution(3048747568265320180)
XLA Ops:
  0.6 0.0 copy-start
  0.6 2.2 %copy-done = bf16[512,4096]{1,0:T(8,128)(2,1)S(1)} copy-done((bf16[512,4096]{1,0:T(8,128)(2,1)S(1)}, bf16[512,4096]{1,0:T(8,128)(2,1)}, u32[]{:S(2)}) %copy-start) | copy-done | bytes 4194328
  2.8 0.0 copy-start.1
  2.8 0.8 %copy-done.1 = bf16[3,4096]{1,0:T(4,128)(2,1)S(1)} copy-done((bf16[3,4096]{1,0:T(4,128)(2,1)S(1)}, bf16[3,4096]{1,0:T(4,128)(2,1)}, u32[]{:S(2)}) %copy-start.1) | copy-done | bytes 24600
  3.6 0.0 copy-start.2
  3.6 0.7 %copy-done.2 = s32[512]{0:T(512)S(1)} copy-done((s32[512]{0:T(512)S(1)}, s32[512]{0:T(512)}, u32[]{:S(2)}) %copy-start.2) | copy-done | bytes 2072
  4.3 0.0 copy-start.3
  4.3 0.7 %copy-done.3 = s32[96]{0:T(128)S(1)} copy-done((s32[96]{0:T(128)S(1)}, s32[96]{0:T(128)}, u32[]{:S(2)}) %copy-start.3) | copy-done | bytes 408
  4.9 24.1 %shard_map.59 = (f32[3,4096]{1,0:T(4,128)S(1)}, f32[1,512]{1,0:T(1,128)S(1)}) custom-call(bf16[512,4096]{1,0:T(8,128)(2,1)S(1)} %copy-done, s32[1,512]{1,0:T(1,128)S(1)} %bitcast.3, s32[1,96]{1,0:T(1,128)S(1)} %bitcast.5, bf16[3,4096]{1,0:T(4,128)(2,1)S(1)} %copy-done.1), custom_call_target="tpu_custom_call" | custom-call | tf_op jit(solution)/shard_map/pallas_call | solution.py:204
  29.1 0.6 %copy.8 = f32[3,4096]{1,0:T(4,128)} copy(f32[3,4096]{1,0:T(4,128)S(1)} %get-tuple-element.8) | data formatting | bytes 98304
  29.7 0.6 %copy.9 = f32[512]{0:T(512)} copy(f32[512]{0:T(512)S(1)} %bitcast.4) | data formatting | bytes 4096
Async XLA Ops:
  0.6 2.2 %copy-start = (bf16[512,4096]{1,0:T(8,128)(2,1)S(1)}, bf16[512,4096]{1,0:T(8,128)(2,1)}, u32[]{:S(2)}) copy-start(bf16[512,4096]{1,0:T(8,128)(2,1)} %emb_hbm.1) | copy-start | bytes 12582916
  2.8 0.8 %copy-start.1 = (bf16[3,4096]{1,0:T(4,128)(2,1)S(1)}, bf16[3,4096]{1,0:T(4,128)(2,1)}, u32[]{:S(2)}) copy-start(bf16[3,4096]{1,0:T(4,128)(2,1)} %cent_ref.1) | copy-start | bytes 73732
  3.6 0.7 %copy-start.2 = (s32[512]{0:T(512)S(1)}, s32[512]{0:T(512)}, u32[]{:S(2)}) copy-start(s32[512]{0:T(512)} %param.5) | copy-start | bytes 6148
  4.3 0.7 %copy-start.3 = (s32[96]{0:T(128)S(1)}, s32[96]{0:T(128)}, u32[]{:S(2)}) copy-start(s32[96]{0:T(128)} %param.6) | copy-start | bytes 1156

commit v2 on v1

--- a/solution.py
+++ b/solution.py
@@ -9,6 +9,7 @@
 
 LANES = 128
 EPS = 1e-06
+VMEM_BYTES = 64 * 1024 * 1024
 
 
 def inner_size(n):
@@ -20,9 +21,9 @@
 
 def kernel(
     n, g, n_clus, nc,
-    emb_hbm, asg_ref, slot_ref, cent_ref, new_ref, dist_ref,
-    emb, sums, recv1, part, recv2, fin, cent_own, cent, cent_wide, cent_mat, sq, mine, theirs,
-    emb_sem, s1_send, s1_recv, s2_send, s2_recv, g1_send, g1_recv, g2_send, g2_recv, x_send, x_recv,
+    emb_hbm, asg_hbm, slot_hbm, cent_hbm, new_ref, dist_ref,
+    asg_ref, slot_ref, cent_ref, emb, sums, recv1, part, recv2, fin, cent_own, cent, cent_wide, cent_mat, sq, mine, theirs,
+    in_sem, emb_sem, s1_send, s1_recv, s2_send, s2_recv, g1_send, g1_recv, g2_send, g2_recv, x_send, x_recv,
 ):
     big = n // g
     rows, width = cent_ref.shape
@@ -39,6 +40,11 @@
     def device(dp):
         return {"dp": dp}
 
+    small = []
+    for i, (src, dst) in enumerate(((cent_hbm, cent_ref), (slot_hbm, slot_ref), (asg_hbm, asg_ref))):
+        cp = pltpu.make_async_copy(src, dst, in_sem.at[i])
+        cp.start()
+        small.append(cp)
     loads = []
     for c in range(nc):
         cols = pl.ds(c * cw, cw)
@@ -64,6 +70,8 @@
         cp.start()
         return cp
 
+    for cp in small:
+        cp.wait()
     old = cent_ref[...].astype(jnp.float32)
     for k in range(tiles):
         cent_own[pl.ds(k, rows, stride=tiles), :] = old[:, k * LANES:(k + 1) * LANES]
@@ -78,28 +86,39 @@
     hot_wide = jnp.dot(place, which, preferred_element_type=jnp.float32)
     hot = hot_wide.astype(jnp.bfloat16)
 
-    pl.semaphore_wait(barrier, len(inner) + len(outer) + len(partners))
-
-    started = []
-    gather1 = [
-        remote(cent.at[p, zo], cent.at[p, zo], g1_send.at[i], g1_recv.at[i], device(d))
-        for i, d in enumerate(outer)
-    ]
-
     span = big * rows * kc
-    step1 = []
-    for c in range(nc):
+
+    def block_sums(c):
         loads[c].wait()
         value = jnp.dot(hot, emb[:, c * cw:(c + 1) * cw], preferred_element_type=jnp.float32)
         for k in range(kc):
             sums[pl.ds(c * block * kc + k, block, stride=kc), :] = value[:, k * LANES:(k + 1) * LANES]
+
+    def send_sums(c):
         copies = []
         for i, d in enumerate(inner):
             start = pl.multiple_of(c * block * kc + lax.rem(p + i + 1, g) * span, 8)
             copies.append(
                 remote(sums.at[pl.ds(start, span)], recv1.at[c, i], s1_send.at[c, i], s1_recv.at[c, i], device(d))
             )
-        step1.append(copies)
+        return copies
+
+    early = nc // 2
+    for c in range(early):
+        block_sums(c)
+
+    pl.semaphore_wait(barrier, len(inner) + len(outer) + len(partners))
+
+    gather1 = [
+        remote(cent.at[p, zo], cent.at[p, zo], g1_send.at[i], g1_recv.at[i], device(d))
+        for i, d in enumerate(outer)
+    ]
+    step1 = [send_sums(c) for c in range(early)]
+    for c in range(early, nc):
+        block_sums(c)
+        step1.append(send_sums(c))
+
+    for c in range(nc):
         x = emb[:, c * cw:(c + 1) * cw].astype(jnp.float32)
         x = x * x
         acc = x[:, :LANES]
@@ -207,9 +226,12 @@
             jax.ShapeDtypeStruct((rows, width), jnp.float32),
             jax.ShapeDtypeStruct((1, points), jnp.float32),
         ),
-        in_specs=[pl.BlockSpec(memory_space=pl.ANY), vmem, vmem, vmem],
+        in_specs=[pl.BlockSpec(memory_space=pltpu.HBM)] * 4,
         out_specs=(vmem, vmem),
         scratch_shapes=[
+            pltpu.VMEM((1, points), jnp.int32),
+            pltpu.VMEM((1, clusters), jnp.int32),
+            pltpu.VMEM((rows, width), old_centroids.dtype),
             pltpu.VMEM((points, width), embeddings.dtype),
             pltpu.VMEM((block * tiles, LANES), jnp.float32),
             pltpu.VMEM((nc, g - 1, big * rows * kc, LANES), jnp.float32),
@@ -223,6 +245,7 @@
             pltpu.VMEM((points, LANES), jnp.float32),
             pltpu.VMEM((8, points), jnp.float32),
             pltpu.VMEM((n_clus - 1, 8, points), jnp.float32),
+            dma((3,)),
             dma((nc,)),
             dma((nc, g - 1)), dma((nc, g - 1)),
             dma((nc, big - 1)), dma((nc, big - 1)),
@@ -231,7 +254,7 @@
             dma((n_clus - 1,)), dma((n_clus - 1,)),
         ],
         compiler_params=pltpu.CompilerParams(
-            collective_id=0, has_side_effects=True, vmem_limit_bytes=48 * 1024 * 1024
+            collective_id=0, has_side_effects=True, vmem_limit_bytes=VMEM_BYTES
         ),
     )(embeddings, assignment.reshape(1, points), slot_of.reshape(1, clusters), old_centroids)
     return new, dist.reshape(points)

time: 30.5 us -> 26.9 us (0.88)
  local copies, waits for them, and re-layouts: 5.48 us -> 2.72 us
  Pallas kernels: 24.1 us -> 23.3 us
    unnamed x10 -> x2, local copies, waits for them, and re-layouts: 5.48 us -> 2.72 us
    pallas_call x1, Pallas kernels: 24.1 us -> 23.3 us  [per_device(): pl.pallas_call(functools.partial(kernel, n, g, n_clus, nc), out_shape=(ja...]
where the time goes in v2:
time: 26.9 us; the launch traced here: 26.7 us
  Pallas kernels  23.3 us (87%)
  local copies, waits for them, and re-layouts  2.72 us (10%)
  between operations  0.64 us (2%)
    pallas_call x1, Pallas kernels, per_device(): pl.pallas_call(functools.partial(kernel, n, g, n_clus, nc), out_shape=(ja...  23.3 us
    unnamed x2, local copies, waits for them, and re-layouts  2.72 us

profile of v2, /device:TPU:0, one launch (start us, length us, event | category | flops | bytes accessed | tf_op | source)
XLA Modules:
  0.0 26.7 jit_solution(17102209117176055637)
XLA Ops:
  0.6 23.3 %shard_map.59 = (f32[3,4096]{1,0:T(4,128)}, f32[1,512]{1,0:T(1,128)}) custom-call(bf16[512,4096]{1,0:T(8,128)(2,1)} %emb_hbm.1, s32[1,512]{1,0:T(1,128)} %bitcast.3, s32[1,96]{1,0:T(1,128)} %bitcast.5, bf16[3,4096]{1,0:T(4,128)(2,1)} %cent_hbm.1), custom_call_target="tpu_custom_call" | custom-call | tf_op jit(solution)/shard_map/pallas_call | solution.py:223
  23.9 1.5 %copy.8 = f32[3,4096]{1,0:T(4,128)} copy(f32[3,4096]{1,0:T(4,128)} %get-tuple-element.8) | data formatting | bytes 98304
  25.4 1.2 %copy.9 = f32[512]{0:T(512)} copy(f32[512]{0:T(512)} %bitcast.4) | data formatting | bytes 4096

commit v3 on v2

--- a/solution.py
+++ b/solution.py
@@ -118,7 +118,7 @@
         block_sums(c)
         step1.append(send_sums(c))
 
-    for c in range(nc):
+    def add_squares(c):
         x = emb[:, c * cw:(c + 1) * cw].astype(jnp.float32)
         x = x * x
         acc = x[:, :LANES]
@@ -129,16 +129,17 @@
         else:
             sq[...] += acc
 
-    for cp in gather1:
-        cp.wait_recv()
-    gather2 = [
-        remote(cent.at[p], cent.at[p], g2_send.at[i], g2_recv.at[i], device(d))
-        for i, d in enumerate(inner)
-    ]
-
     sub = rows * kc
     step2 = []
     for c in range(nc):
+        if c == 1:
+            for cp in gather1:
+                cp.wait_recv()
+            gather2 = [
+                remote(cent.at[p], cent.at[p], g2_send.at[i], g2_recv.at[i], device(d))
+                for i, d in enumerate(inner)
+            ]
+        add_squares(c)
         for cp in step1[c]:
             cp.wait_recv()
         start = pl.multiple_of(c * block * kc + p * span, 8)
@@ -216,7 +217,7 @@
     big = n // g
     block = n * rows
     tiles = width // LANES
-    nc = 4
+    nc = 2
     kc = tiles // nc
     dma = pltpu.SemaphoreType.DMA
     vmem = pl.BlockSpec(memory_space=pltpu.VMEM)

time: 26.9 us -> 26.6 us (0.989)
  no operation moved by 1% of the time
where the time goes in v3:
time: 26.6 us; the launch traced here: 26.4 us
  Pallas kernels  23.1 us (87%)
  local copies, waits for them, and re-layouts  2.72 us (10%)
  between operations  0.64 us (2%)
    pallas_call x1, Pallas kernels, per_device(): pl.pallas_call(functools.partial(kernel, n, g, n_clus, nc), out_shape=(ja...  23.1 us
    unnamed x2, local copies, waits for them, and re-layouts  2.72 us

profile of v3, /device:TPU:0, one launch (start us, length us, event | category | flops | bytes accessed | tf_op | source)
XLA Modules:
  0.0 26.4 jit_solution(1653368076836635107)
XLA Ops:
  0.6 23.1 %shard_map.59 = (f32[3,4096]{1,0:T(4,128)}, f32[1,512]{1,0:T(1,128)}) custom-call(bf16[512,4096]{1,0:T(8,128)(2,1)} %emb_hbm.1, s32[1,512]{1,0:T(1,128)} %bitcast.3, s32[1,96]{1,0:T(1,128)} %bitcast.5, bf16[3,4096]{1,0:T(4,128)(2,1)} %cent_hbm.1), custom_call_target="tpu_custom_call" | custom-call | tf_op jit(solution)/shard_map/pallas_call | solution.py:224
  23.7 1.5 %copy.8 = f32[3,4096]{1,0:T(4,128)} copy(f32[3,4096]{1,0:T(4,128)} %get-tuple-element.8) | data formatting | bytes 98304
  25.2 1.2 %copy.9 = f32[512]{0:T(512)} copy(f32[512]{0:T(512)} %bitcast.4) | data formatting | bytes 4096
